TPU v7x, 32 devices: a whole 2x2x4 slice. The times are simulated.
32 devices in a mesh: parts: 2 (over x), tp: 8 (over z, y), dp: 2 (over core).
Axes of the slice: x: 2, y: 2, z: 4, core: 2. Of those that a mesh axis runs over, the one named last changes fastest.
Arguments:
- tokens: bfloat16 [4, 512, 12288], P(('parts', 'dp'), None, 'tp'), parts along dimension 0, may hold values from -6 to 6
- cotangent: bfloat16 [4, 512, 12288], P(('parts', 'dp'), None, 'tp'), parts along dimension 0, may hold values from -6 to 6
- token_record_index: int32 [4, 512], P(('parts', 'dp')), parts along dimension 0, may hold values from 0 to 3, never falling along the last dimension, each value on 1 to 256 neighbouring positions
- query_weight: bfloat16 [12288, 12288], P('tp'), may hold values from -0.0546875 to 0.0546875
- adapter_down_weight: bfloat16 [12288, 16], P('tp'), may hold values from -0.0546875 to 0.0546875
- adapter_up_weight: bfloat16 [16, 12288], P(None, 'tp'), may hold values from -0.0546875 to 0.0546875
Outputs:
- query: bfloat16 [4, 512, 12288], P(('parts', 'dp'), None, 'tp'), parts along dimension 0
- adapter_a_grad: float32 [32, 12288], P('parts', 'tp'), parts along dimension 0
- adapter_b_grad: float32 [32, 12288], P('parts', 'tp'), parts along dimension 0
There are 2 independent parts, one for each index of `parts`. A program takes and returns all parts, laid end to end along the dimension named above; an argument that names none is the same for every part. Nothing has to cross between parts.
Inputs may be any that keep to these rules, and one draw needn't show every extreme that they name: `token_record_index`: within each pack record numbers never fall, every record 0 to 3 has 1 to 256 tokens, and one record of each pack has exactly 256.
All inputs are finite; a program needn't handle non-finite values.
Results may differ from a plain program's by a relative error of at most 0.0034.
Values may be sent and summed in bfloat16 or wider, within the bound.
A program may use at most 256 MiB of HBM per device.

v0:
```python
import math

import jax
import jax.numpy as jnp
from jax import lax
from jax.sharding import PartitionSpec as P

PACK_RECORDS = 4


ADAPTER_SCALE = 2.0


def spread_matrix(values, record_lookup, record_slots):
    onehot = (record_lookup[:, None] == record_slots[None, :]).astype(jnp.bfloat16)
    return (values[:, None, :] * onehot[:, :, None]).reshape(
        values.shape[0], record_slots.shape[0] * values.shape[1]
    )


def squares(matrix, groups):
    return jnp.sum(jnp.square(matrix.reshape(groups, -1)), axis=1)


def local(
    tokens, cotangent, token_record_index, query_weight, adapter_down_weight, adapter_up_weight
):
    input_features = tokens[0]
    upstream_gradient = cotangent[0]
    record_lookup = token_record_index[0]
    current_pack = record_lookup.shape[0]
    cols = upstream_gradient.shape[1]
    feature_width = query_weight.shape[1]
    rank_width = adapter_down_weight.shape[1]
    record_slots = jnp.arange(PACK_RECORDS, dtype=jnp.int32)
    clipping_limit = ADAPTER_SCALE * math.sqrt(
        2.0 * feature_width * rank_width * current_pack / PACK_RECORDS
    )
    partial_down = jnp.dot(input_features, adapter_down_weight, preferred_element_type=jnp.float32)
    partial_backward = jnp.dot(
        upstream_gradient, adapter_up_weight.T, preferred_element_type=jnp.float32
    )
    down_sum, back_sum = lax.psum((partial_down, partial_backward), "tp")
    down_projected = down_sum.astype(jnp.bfloat16)
    backward_term = back_sum.astype(jnp.bfloat16)
    base_output = lax.psum_scatter(
        lax.dot_general(
            query_weight,
            input_features,
            (((0,), (1,)), ((), ())),
            preferred_element_type=jnp.float32,
        ),
        "tp",
        scatter_dimension=0,
        tiled=True,
    ).T
    adapted_output = jnp.dot(down_projected, adapter_up_weight, preferred_element_type=jnp.float32)
    query = (base_output + ADAPTER_SCALE * adapted_output).astype(jnp.bfloat16)
    down_gradient = ADAPTER_SCALE * jnp.dot(
        spread_matrix(backward_term, record_lookup, record_slots).T,
        input_features,
        preferred_element_type=jnp.float32,
    )
    up_gradient = ADAPTER_SCALE * jnp.dot(
        spread_matrix(down_projected, record_lookup, record_slots).T,
        upstream_gradient,
        preferred_element_type=jnp.float32,
    )
    local_norms = squares(down_gradient, PACK_RECORDS) + squares(up_gradient, PACK_RECORDS)
    norms = lax.psum(local_norms, "tp")
    factor = jnp.minimum(1.0, clipping_limit * lax.rsqrt(norms + 1e-06))
    sum_a = jnp.sum(
        down_gradient.reshape(PACK_RECORDS, rank_width, cols) * factor[:, None, None], axis=0
    )
    sum_b = jnp.sum(
        up_gradient.reshape(PACK_RECORDS, rank_width, cols) * factor[:, None, None], axis=0
    )
    sum_a, sum_b = lax.psum((sum_a, sum_b), "dp")
    scale = 1.0 / (lax.axis_size("dp") * PACK_RECORDS)
    return (query[None], sum_a * scale, sum_b * scale)


def solution(mesh):
    placed = (
        P(("parts", "dp"), None, "tp"),
        P(("parts", "dp"), None, "tp"),
        P(("parts", "dp"), None),
        P("tp", None),
        P("tp", None),
        P(None, "tp"),
    )
    return jax.shard_map(
        local,
        mesh=mesh,
        in_specs=placed,
        out_specs=(P(("parts", "dp"), None, "tp"), P("parts", "tp"), P("parts", "tp")),
        check_vma=False,
    )
```

profile of v0, /device:TPU:0, one launch (start us, length us, event | category | flops | bytes accessed | tf_op | source)
XLA Modules:
  0.0 513.8 jit_solution(10625061380372155697)
XLA Ops:
  8.0 0.0 copy-start
  8.0 0.0 copy-start.3
  8.0 0.0 copy-start.2
  8.0 0.0 all-reduce.4.cloned.1.call-start
  8.1 0.8 fusion.11
  8.9 0.5 copy-done
  9.4 1.3 fusion.7
  10.7 0.0 copy-done.3
  10.7 0.0 copy-done.2
  10.7 0.5 fusion.4
  11.3 39.3 %all-reduce = (bf16[512,16]{0,1:T(8,128)(2,1)S(1)}, bf16[512,16]{0,1:T(8,128)(2,1)S(1)}) all-reduce(f32[512,16]{0,1:T(8,128)S(1)} %fusion.7, f32[512,16]{0,1:T(8,128)S(1)} %fusion.4), channel_id=1, replica_groups=mesh['parts'=2,'tp'=8,'dp'=2] {'tp'}, use_global_device_ids=true, to_apply=%region_1.0 | all-reduce | flops 16384 | bytes 98304 | tf_op jit(solution)/shard_map/psum | solution.py:43
  50.6 1.0 multiply_reduce_fusion.2
  51.6 0.0 copy-start.5
  51.6 0.5 multiply_reduce_fusion.3
  52.1 0.1 reduce_sum.43
  52.2 0.1 copy-done.5
  52.3 0.1 reduce_sum.54
  52.3 0.1 reduce_sum.52
  52.5 0.1 reduce_sum.55
  52.6 17.1 %psum.37 = f32[4]{0:T(128)S(1)} all-reduce(f32[4]{0:T(128)S(1)} %add.22), channel_id=1, replica_groups=mesh['parts'=2,'tp'=8,'dp'=2] {'tp'}, use_global_device_ids=true, to_apply=%region_7.0 | all-reduce | flops 4 | bytes 32 | tf_op jit(solution)/shard_map/psum | solution.py:70
  69.7 0.8 multiply_reduce_fusion
  70.5 0.0 all-reduce.4.cloned.1.call-update
  70.6 0.0 reduce-scatter.2.cloned.1.call-start
  70.6 29.0 %fusion.9 = f32[12288,512]{1,0:T(8,128)} fusion(bf16[1536,12288]{1,0:T(8,128)(2,1)} %param.9, bf16[1,512,1536]{2,1,0:T(8,128)(2,1)S(1)} %copy-done), kind=kOutput, calls=%fused_computation.12 | convolution fusion | flops 19327352832 | bytes 64487424 | tf_op jit(solution)/shard_map/dot_general | solution.py:47
  99.6 0.0 copy-start.4
  99.6 0.0 reduce-scatter.2.cloned.1.call-update
  99.6 0.0 all-reduce.4.cloned.1.call-done
  99.7 1.6 broadcast_multiply_fusion
  101.3 400.8 %reduce-scatter.2.cloned.1.call-done = f32[1536,512]{1,0:T(8,128)} async-done(((f32[12288,512]{1,0:T(8,128)}), f32[1536,512]{1,0:T(8,128)}) %reduce-scatter.2.cloned.1.call-update) | async-done | bytes 3145744 | tf_op jit(solution)/shard_map/reduce_scatter | solution.py:46
  502.1 0.0 copy-done.4
  502.1 0.0 copy-start.1
  502.1 2.6 fusion.2
  504.7 1.6 copy.14
  506.3 0.0 copy-done.1
  (3 shorter events, 0.0 us)
Async XLA Ops:
  8.0 1.4 copy-start
  8.0 2.7 copy-start.3
  8.0 2.7 copy-start.2
  8.0 91.6 %all-reduce.4.cloned.1.call-start = ((), (), s32[]{:S(2)}) async-start(), calls=%async_computation.2 | async-start | bytes 393216 | tf_op jit(solution)/shard_map/psum | solution.py:78
  51.6 0.7 copy-start.5
  70.6 431.6 %reduce-scatter.2.cloned.1.call-start = ((), (), s32[]{:S(2)}) async-start(), calls=%async_computation.1 | async-start | bytes 28311552 | tf_op jit(solution)/shard_map/reduce_scatter | solution.py:46
  99.6 402.5 %copy-start.4 = (bf16[16,1536]{1,0:T(8,128)(2,1)S(1)}, bf16[16,1536]{1,0:T(8,128)(2,1)}, u32[]{:S(2)}) copy-start(bf16[16,1536]{1,0:T(8,128)(2,1)} %param.11) | copy-start | bytes 147460
  502.1 4.2 copy-start.1
Sparse Core Ops, SparseCore 0:
  70.7 16.8 all-reduce.3
Sparse Core Ops, SparseCore 1:
  99.7 402.3 reduce-scatter.1
where the time goes:
time: 514 us
  waiting for transfers between devices  401 us (78%)
  blocking collectives  56.5 us (11%)
  matrix products  34.9 us (7%)
  between operations  15.5 us (3%)
    reduce_scatter x1, waiting for transfers between devices, local(): lax.psum_scatter(lax.dot_general(query_weight, input_features, (((0,), (1...  401 us
    psum x1, blocking collectives, local(): down_sum, back_sum = lax.psum((partial_down, partial_backward), 'tp')  39.3 us
    dot_general x1, matrix products, local(): lax.dot_general(query_weight, input_features, (((0,), (1,)), ((), ())), p...  29 us
    psum x1, blocking collectives, local(): norms = lax.psum(local_norms, 'tp')  17.1 us
  transfers between devices with their start and end apart: 2, of which 1 were waited for; matrix products, arithmetic and copies ran while one was open for 6% of the time, Pallas kernels for 0%

commit v1 on v0

v1 whole, which is shorter than its diff:
```python
import functools
import math

import jax
import jax.numpy as jnp
from jax import lax
from jax.experimental import pallas as pl
from jax.experimental.pallas import tpu as pltpu
from jax.sharding import PartitionSpec as P

PACK_RECORDS = 4
ADAPTER_SCALE = 2.0
W_SLOTS = 4
EARLY = 3


def kernel(
    n_tp, n_dp, clip, cw,
    tok_ref, cot_ref, idx_ref, wq_ref, ad_ref, au_ref,
    query_ref, ga_ref, gb_ref,
    wbuf, ysend, yrecv, acc, zsend, zrecv, small, norms, grad, pair,
    w_sem, ys_sem, yr_sem, zs_sem, zr_sem, ss_sem, sr_sem, ns_sem, nr_sem, ps_sem, pr_sem,
):
    f32, bf16 = jnp.float32, jnp.bfloat16
    tokens, depth = tok_ref.shape
    rank = au_ref.shape[0]
    cols = query_ref.shape[1]
    subs = cols // cw
    n_z = n_tp // 2
    items = n_z * subs
    me = lax.axis_index("tp")
    core = lax.axis_index("dp")
    my_z, my_y = me // 2, lax.rem(me, 2)
    other_y = 1 - my_y
    partner = my_z * 2 + other_y

    def dest_z(item):
        step = item // subs
        order = jnp.where(step == n_z - 1, 0, lax.rem(step + n_z // 2, n_z))
        order = jnp.where((step >= n_z // 2) & (step < n_z - 1), step - n_z // 2 + 1, order)
        return lax.rem(my_z + order, n_z)

    def w_copy(step):
        half = step // items
        item = lax.rem(step, items)
        y = jnp.where(half == 0, other_y, my_y)
        col = (dest_z(item) * 2 + y) * cols + lax.rem(item, subs) * cw
        slot = lax.rem(step, W_SLOTS)
        return pltpu.make_async_copy(
            wq_ref.at[:, pl.ds(pl.multiple_of(col, 128), cw)], wbuf.at[slot], w_sem.at[slot]
        )

    def product(step):
        w_copy(step).wait()
        return jnp.dot(tok_ref[...], wbuf[lax.rem(step, W_SLOTS)], preferred_element_type=f32)

    def prefetch(step):
        @pl.when(step + W_SLOTS < 2 * items)
        def _():
            w_copy(step + W_SLOTS).start()

    def y_copy(item):
        return pltpu.make_async_remote_copy(
            src_ref=ysend.at[item], dst_ref=yrecv.at[item],
            send_sem=ys_sem.at[item], recv_sem=yr_sem.at[item],
            device_id={"tp": partner}, device_id_type=pl.DeviceIdType.MESH,
        )

    def z_copy(item):
        sub = lax.rem(item, subs)
        return pltpu.make_async_remote_copy(
            src_ref=zsend.at[item], dst_ref=zrecv.at[my_z * subs + sub],
            send_sem=zs_sem.at[item], recv_sem=zr_sem.at[my_z * subs + sub],
            device_id={"tp": dest_z(item) * 2 + my_y}, device_id_type=pl.DeviceIdType.MESH,
        )

    def z_arrival(slot):
        return pltpu.make_async_remote_copy(
            src_ref=zrecv.at[slot], dst_ref=zrecv.at[slot],
            send_sem=zs_sem.at[0], recv_sem=zr_sem.at[slot],
            device_id={"tp": partner}, device_id_type=pl.DeviceIdType.MESH,
        )

    def share(buf, slot, peer, send, recv):
        return pltpu.make_async_remote_copy(
            src_ref=buf.at[slot], dst_ref=buf.at[slot],
            send_sem=send.at[peer], recv_sem=recv.at[slot],
            device_id={"tp": peer}, device_id_type=pl.DeviceIdType.MESH,
        )

    def over_peers(fn):
        def body(j, carry):
            fn(lax.rem(me + j, n_tp))
            return carry

        lax.fori_loop(1, n_tp, body, 0)

    for step in range(W_SLOTS):
        w_copy(step).start()

    barrier = pltpu.get_barrier_semaphore()
    over_peers(lambda peer: pl.semaphore_signal(
        barrier, inc=1, device_id={"tp": peer}, device_id_type=pl.DeviceIdType.MESH))
    for d in range(1, n_dp):
        pl.semaphore_signal(
            barrier, inc=1, device_id={"dp": lax.rem(core + d, n_dp)},
            device_id_type=pl.DeviceIdType.MESH)
    pl.semaphore_wait(barrier, n_tp + n_dp - 2)

    nt = (((1,), (1,)), ((), ()))
    small[me, pl.ds(0, rank), :] = lax.dot_general(
        ad_ref[...], tok_ref[...], nt, preferred_element_type=f32)
    small[me, pl.ds(rank, rank), :] = lax.dot_general(
        au_ref[...], cot_ref[...], nt, preferred_element_type=f32)
    over_peers(lambda peer: share(small, me, peer, ss_sem, sr_sem).start())

    def y_step(item, carry):
        ysend[item] = product(item).astype(bf16)
        y_copy(item).start()
        prefetch(item)
        return carry

    early = min(EARLY, items)
    lax.fori_loop(0, early, y_step, 0)

    over_peers(lambda peer: share(small, peer, peer, ss_sem, sr_sem).wait_recv())
    total = small[0]
    for j in range(1, n_tp):
        total = total + small[j]
    down = total[:rank].astype(bf16)
    back = total[rank:].astype(bf16)
    record = idx_ref[...]

    def spread(values):
        return jnp.concatenate(
            [jnp.where(record == r, values, jnp.zeros_like(values)) for r in range(PACK_RECORDS)],
            axis=0,
        )

    grad[0] = ADAPTER_SCALE * jnp.dot(spread(back), tok_ref[...], preferred_element_type=f32)
    grad[1] = ADAPTER_SCALE * jnp.dot(spread(down), cot_ref[...], preferred_element_type=f32)
    for r in range(PACK_RECORDS):
        rows = pl.ds(r * rank, rank)
        ga, gb = grad[0, rows, :], grad[1, rows, :]
        square = jnp.sum(jnp.sum(ga * ga + gb * gb, axis=0, keepdims=True), axis=1, keepdims=True)
        norms[me, pl.ds(r * 8, 8), :] = jnp.broadcast_to(square, (8, 128))
    over_peers(lambda peer: share(norms, me, peer, ns_sem, nr_sem).start())

    lax.fori_loop(early, items, y_step, 0)

    def own_step(item, carry):
        acc[item] = product(item + items)
        prefetch(item + items)
        return carry

    lax.fori_loop(0, items, own_step, 0)

    own0 = items - subs
    lanes = down.astype(f32).T.astype(bf16)
    for sub in range(subs):
        acc[own0 + sub] += ADAPTER_SCALE * jnp.dot(
            lanes, au_ref[:, pl.ds(sub * cw, cw)], preferred_element_type=f32)

    over_peers(lambda peer: share(norms, peer, peer, ns_sem, nr_sem).wait_recv())
    norm = norms[0]
    for j in range(1, n_tp):
        norm = norm + norms[j]
    factor = jnp.minimum(1.0, clip * lax.rsqrt(norm + 1e-06))
    for side in range(2):
        part = jnp.zeros((rank, cols), f32)
        for r in range(PACK_RECORDS):
            part = part + grad[side, pl.ds(r * rank, rank), :] * factor[r * 8:r * 8 + 1, 0:1]
        pair[core, pl.ds(side * rank, rank), :] = part

    def pair_copy(slot, other):
        return pltpu.make_async_remote_copy(
            src_ref=pair.at[slot], dst_ref=pair.at[slot],
            send_sem=ps_sem.at[other], recv_sem=pr_sem.at[slot],
            device_id={"dp": other}, device_id_type=pl.DeviceIdType.MESH,
        )

    for d in range(1, n_dp):
        pair_copy(core, lax.rem(core + d, n_dp)).start()

    def z_step(item, carry):
        y_copy(item).wait_recv()
        zsend[item] = (acc[item] + yrecv[item].astype(f32)).astype(bf16)
        z_copy(item).start()
        return carry

    lax.fori_loop(0, own0, z_step, 0)

    for d in range(1, n_dp):
        other = lax.rem(core + d, n_dp)
        pair_copy(other, other).wait_recv()
    both = pair[0]
    for d in range(1, n_dp):
        both = both + pair[d]
    scale = 1.0 / (n_dp * PACK_RECORDS)
    ga_ref[...] = both[:rank] * scale
    gb_ref[...] = both[rank:] * scale

    def own_sum(item, carry):
        y_copy(item).wait_recv()
        acc[item] += yrecv[item].astype(f32)
        return carry

    lax.fori_loop(own0, items, own_sum, 0)

    for sub in range(subs):
        def arrive(j, carry):
            slot = lax.rem(my_z + j, n_z) * subs + sub
            z_arrival(slot).wait_recv()
            acc[own0 + sub] += zrecv[slot].astype(f32)
            return carry

        lax.fori_loop(1, n_z, arrive, 0)
        query_ref[:, pl.ds(sub * cw, cw)] = acc[own0 + sub].astype(bf16)

    def y_done(item, carry):
        y_copy(item).wait_send()
        return carry

    lax.fori_loop(0, items, y_done, 0)

    def z_done(item, carry):
        z_copy(item).wait_send()
        return carry

    lax.fori_loop(0, own0, z_done, 0)
    over_peers(lambda peer: share(small, me, peer, ss_sem, sr_sem).wait_send())
    over_peers(lambda peer: share(norms, me, peer, ns_sem, nr_sem).wait_send())
    for d in range(1, n_dp):
        pair_copy(core, lax.rem(core + d, n_dp)).wait_send()


def local(n_tp, n_dp, tokens, cotangent, index, query_weight, down_weight, up_weight):
    f32, bf16 = jnp.float32, jnp.bfloat16
    rows, depth = tokens.shape[1:]
    rank, cols = up_weight.shape
    width = query_weight.shape[1]
    clip = ADAPTER_SCALE * math.sqrt(2.0 * width * rank * rows / PACK_RECORDS)
    cw = 512 if cols % 512 == 0 else cols
    subs = cols // cw
    n_z = n_tp // 2
    items = n_z * subs
    dma = pltpu.SemaphoreType.DMA
    vmem = pl.BlockSpec(memory_space=pltpu.VMEM)
    query, grad_a, grad_b = pl.pallas_call(
        functools.partial(kernel, n_tp, n_dp, clip, cw),
        out_shape=(
            jax.ShapeDtypeStruct((rows, cols), bf16),
            jax.ShapeDtypeStruct((rank, cols), f32),
            jax.ShapeDtypeStruct((rank, cols), f32),
        ),
        in_specs=[vmem, vmem, vmem, pl.BlockSpec(memory_space=pl.ANY), vmem, vmem],
        out_specs=(vmem, vmem, vmem),
        scratch_shapes=[
            pltpu.VMEM((W_SLOTS, depth, cw), bf16),
            pltpu.VMEM((items, rows, cw), bf16),
            pltpu.VMEM((items, rows, cw), bf16),
            pltpu.VMEM((items, rows, cw), f32),
            pltpu.VMEM((items - subs, rows, cw), bf16),
            pltpu.VMEM((items, rows, cw), bf16),
            pltpu.VMEM((n_tp, 2 * rank, rows), f32),
            pltpu.VMEM((n_tp, 8 * PACK_RECORDS, 128), f32),
            pltpu.VMEM((2, PACK_RECORDS * rank, cols), f32),
            pltpu.VMEM((n_dp, 2 * rank, cols), f32),
            dma((W_SLOTS,)),
            dma((items,)),
            dma((items,)),
            dma((items,)),
            dma((items,)),
            dma((n_tp,)),
            dma((n_tp,)),
            dma((n_tp,)),
            dma((n_tp,)),
            dma((n_dp,)),
            dma((n_dp,)),
        ],
        compiler_params=pltpu.CompilerParams(
            collective_id=0, has_side_effects=True, vmem_limit_bytes=60 * 1024 * 1024),
        cost_estimate=pl.CostEstimate(
            flops=2 * rows * depth * width, bytes_accessed=2 * depth * width, transcendentals=0),
    )(tokens[0], cotangent[0], index, query_weight, down_weight.T, up_weight)
    return query[None], grad_a, grad_b


def solution(mesh):
    placed = (
        P(("parts", "dp"), None, "tp"),
        P(("parts", "dp"), None, "tp"),
        P(("parts", "dp"), None),
        P("tp", None),
        P("tp", None),
        P(None, "tp"),
    )
    return jax.shard_map(
        functools.partial(local, mesh.shape["tp"], mesh.shape["dp"]),
        mesh=mesh,
        in_specs=placed,
        out_specs=(P(("parts", "dp"), None, "tp"), P("parts", "tp"), P("parts", "tp")),
        check_vma=False,
    )
```

time: 514 us -> 192 us (0.37)
  the two profiles are of different devices: /device:TPU:0 before, /device:TPU:13 now
where the time goes in v1:
time: 192 us
  Pallas kernels  187 us (97%)
  local copies, waits for them, and re-layouts  3.98 us (2%)
    pallas_call x1, Pallas kernels, local(): pl.pallas_call(functools.partial(kernel, n_tp, n_dp, clip, cw), out_shape...  187 us
    unnamed x7, local copies, waits for them, and re-layouts  3.98 us

profile of v1, /device:TPU:13, one launch (start us, length us, event | category | flops | bytes accessed | tf_op | source)
XLA Modules:
  0.0 191.5 jit_solution(15934687648703329253)
XLA Ops:
  0.6 186.9 %shard_map.85 = (bf16[512,1536]{1,0:T(8,128)(2,1)}, f32[16,1536]{1,0:T(8,128)}, f32[16,1536]{1,0:T(8,128)}) custom-call(bf16[512,1536]{1,0:T(8,128)(2,1)} %bitcast.5, bf16[512,1536]{1,0:T(8,128)(2,1)} %bitcast.6, s32[1,512]{1,0:T(1,128)} %idx_ref.1, bf16[1536,12288]{1,0:T(8,128)(2,1)} %wq_ref.1, bf16[16,1536]{1,0:T(8,128)(2,1)} %bitcast.7, ...), custom_call_target="tpu_custom_call" | custom-call | flops 19327352832 | bytes 37748736 | tf_op jit(solution)/shard_map/pallas_call | solution.py:249
  187.5 0.0 copy-start.1
  187.5 0.0 copy-start
  187.5 2.7 %copy.12 = bf16[1,512,1536]{2,1,0:T(8,128)(2,1)} copy(bf16[1,512,1536]{2,1,0:T(8,128)(2,1)} %bitcast.4) | data formatting | bytes 3145728
  190.2 0.0 copy-done.1
  190.2 0.6 copy.13
  190.9 0.0 copy-done
  190.9 0.6 copy.14
Async XLA Ops:
  187.5 2.7 %copy-start.1 = (f32[16,1536]{1,0:T(8,128)S(1)}, f32[16,1536]{1,0:T(8,128)}, u32[]{:S(2)}) copy-start(f32[16,1536]{1,0:T(8,128)} %get-tuple-element.13) | copy-start | bytes 294916
  187.5 3.3 %copy-start = (f32[16,1536]{1,0:T(8,128)S(1)}, f32[16,1536]{1,0:T(8,128)}, u32[]{:S(2)}) copy-start(f32[16,1536]{1,0:T(8,128)} %get-tuple-element.14) | copy-start | bytes 294916

commit v2 on v1

--- a/solution.py
+++ b/solution.py
@@ -12,39 +12,46 @@
 ADAPTER_SCALE = 2.0
 W_SLOTS = 4
 EARLY = 3
+AHEAD = 2
+P_FIRST = 1
 
 
 def kernel(
     n_tp, n_dp, clip, cw,
     tok_ref, cot_ref, idx_ref, wq_ref, ad_ref, au_ref,
     query_ref, ga_ref, gb_ref,
-    wbuf, ysend, yrecv, acc, zsend, zrecv, small, norms, grad, pair,
-    w_sem, ys_sem, yr_sem, zs_sem, zr_sem, ss_sem, sr_sem, ns_sem, nr_sem, ps_sem, pr_sem,
+    wbuf, send1, recv1, acc, send2, recv2, send3, recv3, small, norms, grad, pair,
+    w_sem, s1_sem, r1_sem, s2_sem, r2_sem, s3_sem, r3_sem, ss_sem, sr_sem, ns_sem, nr_sem, ps_sem, pr_sem,
 ):
     f32, bf16 = jnp.float32, jnp.bfloat16
     tokens, depth = tok_ref.shape
     rank = au_ref.shape[0]
     cols = query_ref.shape[1]
     subs = cols // cw
-    n_z = n_tp // 2
-    items = n_z * subs
+    n_h = n_tp // 4
+    items = 2 * n_h * subs
     me = lax.axis_index("tp")
     core = lax.axis_index("dp")
-    my_z, my_y = me // 2, lax.rem(me, 2)
-    other_y = 1 - my_y
-    partner = my_z * 2 + other_y
-
-    def dest_z(item):
-        step = item // subs
-        order = jnp.where(step == n_z - 1, 0, lax.rem(step + n_z // 2, n_z))
-        order = jnp.where((step >= n_z // 2) & (step < n_z - 1), step - n_z // 2 + 1, order)
-        return lax.rem(my_z + order, n_z)
+    my_h, my_p, my_y = me // 4, lax.rem(me // 2, 2), lax.rem(me, 2)
+    y_mate = me + 1 - 2 * my_y
+    p_mate = me + 2 - 4 * my_p
+
+    def dest_h(hi):
+        return lax.rem(my_h + hi + 1, n_h)
+
+    def at(hi, pi, s):
+        return (hi * 2 + pi) * subs + s
 
     def w_copy(step):
-        half = step // items
+        own = step // items
         item = lax.rem(step, items)
-        y = jnp.where(half == 0, other_y, my_y)
-        col = (dest_z(item) * 2 + y) * cols + lax.rem(item, subs) * cw
+        s = lax.rem(item, subs)
+        pi = lax.rem(item // subs, 2)
+        hi = item // (2 * subs)
+        p_first = s < P_FIRST
+        y = jnp.where(jnp.where(p_first, pi, own) == 1, my_y, 1 - my_y)
+        p = jnp.where(jnp.where(p_first, own, pi) == 1, my_p, 1 - my_p)
+        col = (dest_h(hi) * 4 + p * 2 + y) * cols + s * cw
         slot = lax.rem(step, W_SLOTS)
         return pltpu.make_async_copy(
             wq_ref.at[:, pl.ds(pl.multiple_of(col, 128), cw)], wbuf.at[slot], w_sem.at[slot]
@@ -59,26 +66,39 @@
         def _():
             w_copy(step + W_SLOTS).start()
 
-    def y_copy(item):
-        return pltpu.make_async_remote_copy(
-            src_ref=ysend.at[item], dst_ref=yrecv.at[item],
-            send_sem=ys_sem.at[item], recv_sem=yr_sem.at[item],
-            device_id={"tp": partner}, device_id_type=pl.DeviceIdType.MESH,
-        )
-
-    def z_copy(item):
-        sub = lax.rem(item, subs)
-        return pltpu.make_async_remote_copy(
-            src_ref=zsend.at[item], dst_ref=zrecv.at[my_z * subs + sub],
-            send_sem=zs_sem.at[item], recv_sem=zr_sem.at[my_z * subs + sub],
-            device_id={"tp": dest_z(item) * 2 + my_y}, device_id_type=pl.DeviceIdType.MESH,
-        )
-
-    def z_arrival(slot):
-        return pltpu.make_async_remote_copy(
-            src_ref=zrecv.at[slot], dst_ref=zrecv.at[slot],
-            send_sem=zs_sem.at[0], recv_sem=zr_sem.at[slot],
-            device_id={"tp": partner}, device_id_type=pl.DeviceIdType.MESH,
+    def first_copy(item):
+        s = lax.rem(item, subs)
+        return pltpu.make_async_remote_copy(
+            src_ref=send1.at[item], dst_ref=recv1.at[item],
+            send_sem=s1_sem.at[item], recv_sem=r1_sem.at[item],
+            device_id={"tp": jnp.where(s < P_FIRST, p_mate, y_mate)},
+            device_id_type=pl.DeviceIdType.MESH,
+        )
+
+    def second_copy(hi, s):
+        i = hi * subs + s
+        return pltpu.make_async_remote_copy(
+            src_ref=send2.at[i], dst_ref=recv2.at[i],
+            send_sem=s2_sem.at[i], recv_sem=r2_sem.at[i],
+            device_id={"tp": jnp.where(s < P_FIRST, y_mate, p_mate)},
+            device_id_type=pl.DeviceIdType.MESH,
+        )
+
+    def third_copy(hi, s):
+        i = hi * subs + s
+        return pltpu.make_async_remote_copy(
+            src_ref=send3.at[i], dst_ref=recv3.at[my_h * subs + s],
+            send_sem=s3_sem.at[i], recv_sem=r3_sem.at[my_h * subs + s],
+            device_id={"tp": dest_h(hi) * 4 + my_p * 2 + my_y},
+            device_id_type=pl.DeviceIdType.MESH,
+        )
+
+    def third_arrival(h, s):
+        i = h * subs + s
+        return pltpu.make_async_remote_copy(
+            src_ref=recv3.at[i], dst_ref=recv3.at[i],
+            send_sem=s3_sem.at[0], recv_sem=r3_sem.at[i],
+            device_id={"tp": y_mate}, device_id_type=pl.DeviceIdType.MESH,
         )
 
     def share(buf, slot, peer, send, recv):
@@ -114,14 +134,18 @@
         au_ref[...], cot_ref[...], nt, preferred_element_type=f32)
     over_peers(lambda peer: share(small, me, peer, ss_sem, sr_sem).start())
 
-    def y_step(item, carry):
-        ysend[item] = product(item).astype(bf16)
-        y_copy(item).start()
+    def first_step(item, carry):
+        send1[item] = product(item).astype(bf16)
+
+        @pl.when((item < AHEAD * subs) | (lax.rem(item, subs) < P_FIRST))
+        def _():
+            first_copy(item).start()
+
         prefetch(item)
         return carry
 
     early = min(EARLY, items)
-    lax.fori_loop(0, early, y_step, 0)
+    lax.fori_loop(0, early, first_step, 0)
 
     over_peers(lambda peer: share(small, peer, peer, ss_sem, sr_sem).wait_recv())
     total = small[0]
@@ -146,7 +170,7 @@
         norms[me, pl.ds(r * 8, 8), :] = jnp.broadcast_to(square, (8, 128))
     over_peers(lambda peer: share(norms, me, peer, ns_sem, nr_sem).start())
 
-    lax.fori_loop(early, items, y_step, 0)
+    lax.fori_loop(early, items, first_step, 0)
 
     def own_step(item, carry):
         acc[item] = product(item + items)
@@ -155,7 +179,7 @@
 
     lax.fori_loop(0, items, own_step, 0)
 
-    own0 = items - subs
+    own0 = at(n_h - 1, 1, 0)
     lanes = down.astype(f32).T.astype(bf16)
     for sub in range(subs):
         acc[own0 + sub] += ADAPTER_SCALE * jnp.dot(
@@ -182,13 +206,57 @@
     for d in range(1, n_dp):
         pair_copy(core, lax.rem(core + d, n_dp)).start()
 
-    def z_step(item, carry):
-        y_copy(item).wait_recv()
-        zsend[item] = (acc[item] + yrecv[item].astype(f32)).astype(bf16)
-        z_copy(item).start()
-        return carry
-
-    lax.fori_loop(0, own0, z_step, 0)
+    def add_first(hi, pi, s):
+        item = at(hi, pi, s)
+        first_copy(item).wait_recv()
+        return acc[item] + recv1[item].astype(f32)
+
+    def pass_second(hi, s):
+        send2[hi * subs + s] = add_first(hi, 0, s).astype(bf16)
+        second_copy(hi, s).start()
+
+    def add_second(hi, s, value):
+        second_copy(hi, s).wait_recv()
+        return value + recv2[hi * subs + s].astype(f32)
+
+    def pass_third(hi, s, value):
+        send3[hi * subs + s] = value.astype(bf16)
+        third_copy(hi, s).start()
+
+    def more(hi, pi, s):
+        nxt = at(hi, pi, s) + AHEAD * subs
+
+        @pl.when(nxt < items)
+        def _():
+            first_copy(nxt).start()
+
+    def p_first_step(hi, carry):
+        for s in range(P_FIRST):
+            pass_second(hi, s)
+            acc[at(hi, 1, s)] = add_first(hi, 1, s)
+        return carry
+
+    lax.fori_loop(0, n_h, p_first_step, 0)
+
+    def far_step(hi, carry):
+        def other_place(s, c):
+            pass_second(hi, s)
+            more(hi, 0, s)
+            return c
+
+        def own_place(s, c):
+            value = add_first(hi, 1, s)
+            more(hi, 1, s)
+            pass_third(hi, s, add_second(hi, s, value))
+            return c
+
+        lax.fori_loop(P_FIRST, subs, other_place, 0)
+        lax.fori_loop(P_FIRST, subs, own_place, 0)
+        for s in range(P_FIRST):
+            pass_third(hi, s, add_second(hi, s, acc[at(hi, 1, s)]))
+        return carry
+
+    lax.fori_loop(0, n_h - 1, far_step, 0)
 
     for d in range(1, n_dp):
         other = lax.rem(core + d, n_dp)
@@ -200,34 +268,44 @@
     ga_ref[...] = both[:rank] * scale
     gb_ref[...] = both[rank:] * scale
 
-    def own_sum(item, carry):
-        y_copy(item).wait_recv()
-        acc[item] += yrecv[item].astype(f32)
-        return carry
-
-    lax.fori_loop(own0, items, own_sum, 0)
-
-    for sub in range(subs):
+    last = n_h - 1
+
+    def last_other(s, carry):
+        pass_second(last, s)
+        return carry
+
+    lax.fori_loop(P_FIRST, subs, last_other, 0)
+
+    for s in range(subs):
+        value = acc[own0 + s] if s < P_FIRST else add_first(last, 1, s)
+        acc[own0 + s] = add_second(last, s, value)
+
         def arrive(j, carry):
-            slot = lax.rem(my_z + j, n_z) * subs + sub
-            z_arrival(slot).wait_recv()
-            acc[own0 + sub] += zrecv[slot].astype(f32)
+            h = lax.rem(my_h + j, n_h)
+            third_arrival(h, s).wait_recv()
+            acc[own0 + s] += recv3[h * subs + s].astype(f32)
             return carry
 
-        lax.fori_loop(1, n_z, arrive, 0)
-        query_ref[:, pl.ds(sub * cw, cw)] = acc[own0 + sub].astype(bf16)
-
-    def y_done(item, carry):
-        y_copy(item).wait_send()
-        return carry
-
-    lax.fori_loop(0, items, y_done, 0)
-
-    def z_done(item, carry):
-        z_copy(item).wait_send()
-        return carry
-
-    lax.fori_loop(0, own0, z_done, 0)
+        lax.fori_loop(1, n_h, arrive, 0)
+        query_ref[:, pl.ds(s * cw, cw)] = acc[own0 + s].astype(bf16)
+
+    def first_done(item, carry):
+        first_copy(item).wait_send()
+        return carry
+
+    lax.fori_loop(0, items, first_done, 0)
+
+    def second_done(i, carry):
+        second_copy(i // subs, lax.rem(i, subs)).wait_send()
+        return carry
+
+    lax.fori_loop(0, n_h * subs, second_done, 0)
+
+    def third_done(i, carry):
+        third_copy(i // subs, lax.rem(i, subs)).wait_send()
+        return carry
+
+    lax.fori_loop(0, last * subs, third_done, 0)
     over_peers(lambda peer: share(small, me, peer, ss_sem, sr_sem).wait_send())
     over_peers(lambda peer: share(norms, me, peer, ns_sem, nr_sem).wait_send())
     for d in range(1, n_dp):
@@ -240,10 +318,10 @@
     rank, cols = up_weight.shape
     width = query_weight.shape[1]
     clip = ADAPTER_SCALE * math.sqrt(2.0 * width * rank * rows / PACK_RECORDS)
-    cw = 512 if cols % 512 == 0 else cols
-    subs = cols // cw
-    n_z = n_tp // 2
-    items = n_z * subs
+    subs = 4 if cols % 512 == 0 else 3
+    cw = cols // subs
+    n_h = n_tp // 4
+    items = 2 * n_h * subs
     dma = pltpu.SemaphoreType.DMA
     vmem = pl.BlockSpec(memory_space=pltpu.VMEM)
     query, grad_a, grad_b = pl.pallas_call(
@@ -260,8 +338,10 @@
             pltpu.VMEM((items, rows, cw), bf16),
             pltpu.VMEM((items, rows, cw), bf16),
             pltpu.VMEM((items, rows, cw), f32),
-            pltpu.VMEM((items - subs, rows, cw), bf16),
-            pltpu.VMEM((items, rows, cw), bf16),
+            pltpu.VMEM((n_h * subs, rows, cw), bf16),
+            pltpu.VMEM((n_h * subs, rows, cw), bf16),
+            pltpu.VMEM(((n_h - 1) * subs, rows, cw), bf16),
+            pltpu.VMEM((n_h * subs, rows, cw), bf16),
             pltpu.VMEM((n_tp, 2 * rank, rows), f32),
             pltpu.VMEM((n_tp, 8 * PACK_RECORDS, 128), f32),
             pltpu.VMEM((2, PACK_RECORDS * rank, cols), f32),
@@ -269,8 +349,10 @@
             dma((W_SLOTS,)),
             dma((items,)),
             dma((items,)),
-            dma((items,)),
-            dma((items,)),
+            dma((n_h * subs,)),
+            dma((n_h * subs,)),
+            dma(((n_h - 1) * subs,)),
+            dma((n_h * subs,)),
             dma((n_tp,)),
             dma((n_tp,)),
             dma((n_tp,)),

time: 192 us -> 147 us (0.77)
  the two profiles are of different devices: /device:TPU:13 before, /device:TPU:0 now
where the time goes in v2:
time: 147 us
  Pallas kernels  143 us (97%)
  local copies, waits for them, and re-layouts  3.98 us (3%)
    pallas_call x1, Pallas kernels, local(): pl.pallas_call(functools.partial(kernel, n_tp, n_dp, clip, cw), out_shape...  143 us
    unnamed x7, local copies, waits for them, and re-layouts  3.98 us

profile of v2, /device:TPU:0, one launch (start us, length us, event | category | flops | bytes accessed | tf_op | source)
XLA Modules:
  0.0 147.2 jit_solution(15832529197504344410)
XLA Ops:
  0.6 142.6 %shard_map.85 = (bf16[512,1536]{1,0:T(8,128)(2,1)}, f32[16,1536]{1,0:T(8,128)}, f32[16,1536]{1,0:T(8,128)}) custom-call(bf16[512,1536]{1,0:T(8,128)(2,1)} %bitcast.5, bf16[512,1536]{1,0:T(8,128)(2,1)} %bitcast.6, s32[1,512]{1,0:T(1,128)} %idx_ref.1, bf16[1536,12288]{1,0:T(8,128)(2,1)} %wq_ref.1, bf16[16,1536]{1,0:T(8,128)(2,1)} %bitcast.7, ...), custom_call_target="tpu_custom_call" | custom-call | flops 19327352832 | bytes 37748736 | tf_op jit(solution)/shard_map/pallas_call | solution.py:327
  143.2 0.0 copy-start.1
  143.3 0.0 copy-start
  143.3 2.7 %copy.12 = bf16[1,512,1536]{2,1,0:T(8,128)(2,1)} copy(bf16[1,512,1536]{2,1,0:T(8,128)(2,1)} %bitcast.4) | data formatting | bytes 3145728
  146.0 0.0 copy-done.1
  146.0 0.6 copy.13
  146.6 0.0 copy-done
  146.6 0.6 copy.14
Async XLA Ops:
  143.2 2.7 %copy-start.1 = (f32[16,1536]{1,0:T(8,128)S(1)}, f32[16,1536]{1,0:T(8,128)}, u32[]{:S(2)}) copy-start(f32[16,1536]{1,0:T(8,128)} %get-tuple-element.13) | copy-start | bytes 294916
  143.3 3.3 %copy-start = (f32[16,1536]{1,0:T(8,128)S(1)}, f32[16,1536]{1,0:T(8,128)}, u32[]{:S(2)}) copy-start(f32[16,1536]{1,0:T(8,128)} %get-tuple-element.14) | copy-start | bytes 294916

commit v3 on v2

--- a/solution.py
+++ b/solution.py
@@ -29,7 +29,8 @@
     cols = query_ref.shape[1]
     subs = cols // cw
     n_h = n_tp // 4
-    items = 2 * n_h * subs
+    group = 2 * subs
+    items = n_h * group
     me = lax.axis_index("tp")
     core = lax.axis_index("dp")
     my_h, my_p, my_y = me // 4, lax.rem(me // 2, 2), lax.rem(me, 2)
@@ -43,8 +44,10 @@
         return (hi * 2 + pi) * subs + s
 
     def w_copy(step):
-        own = step // items
-        item = lax.rem(step, items)
+        early, middle, late = step < group, step < items, step < 2 * items - group
+        own = jnp.where(early | (jnp.logical_not(middle) & late), 0, 1)
+        item = step - jnp.where(
+            early, 0, jnp.where(middle, group, jnp.where(late, items - group, items)))
         s = lax.rem(item, subs)
         pi = lax.rem(item // subs, 2)
         hi = item // (2 * subs)
@@ -135,17 +138,23 @@
     over_peers(lambda peer: share(small, me, peer, ss_sem, sr_sem).start())
 
     def first_step(item, carry):
-        send1[item] = product(item).astype(bf16)
+        step = jnp.where(item < group, item, item + items - group)
+        send1[item] = product(step).astype(bf16)
 
         @pl.when((item < AHEAD * subs) | (lax.rem(item, subs) < P_FIRST))
         def _():
             first_copy(item).start()
 
-        prefetch(item)
-        return carry
-
-    early = min(EARLY, items)
-    lax.fori_loop(0, early, first_step, 0)
+        prefetch(step)
+        return carry
+
+    def own_step(item, carry):
+        step = jnp.where(item < items - group, item + group, item + items)
+        acc[item] = product(step)
+        prefetch(step)
+        return carry
+
+    lax.fori_loop(0, EARLY, first_step, 0)
 
     over_peers(lambda peer: share(small, peer, peer, ss_sem, sr_sem).wait_recv())
     total = small[0]
@@ -170,14 +179,54 @@
         norms[me, pl.ds(r * 8, 8), :] = jnp.broadcast_to(square, (8, 128))
     over_peers(lambda peer: share(norms, me, peer, ns_sem, nr_sem).start())
 
-    lax.fori_loop(early, items, first_step, 0)
-
-    def own_step(item, carry):
-        acc[item] = product(item + items)
-        prefetch(item + items)
-        return carry
-
-    lax.fori_loop(0, items, own_step, 0)
+    lax.fori_loop(EARLY, group, first_step, 0)
+    lax.fori_loop(0, items - group, own_step, 0)
+    lax.fori_loop(group, items, first_step, 0)
+
+    def add_first(hi, pi, s):
+        item = at(hi, pi, s)
+        first_copy(item).wait_recv()
+        return acc[item] + recv1[item].astype(f32)
+
+    def pass_second(hi, s):
+        send2[hi * subs + s] = add_first(hi, 0, s).astype(bf16)
+        second_copy(hi, s).start()
+
+    def add_second(hi, s, value):
+        second_copy(hi, s).wait_recv()
+        return value + recv2[hi * subs + s].astype(f32)
+
+    def pass_third(hi, s, value):
+        send3[hi * subs + s] = value.astype(bf16)
+        third_copy(hi, s).start()
+
+    def more(hi, pi, s):
+        nxt = at(hi, pi, s) + AHEAD * subs
+
+        @pl.when(nxt < items)
+        def _():
+            first_copy(nxt).start()
+
+    def p_first_step(hi, carry):
+        for s in range(P_FIRST):
+            pass_second(hi, s)
+            acc[at(hi, 1, s)] = add_first(hi, 1, s)
+        return carry
+
+    def other_place(hi):
+        def body(s, carry):
+            pass_second(hi, s)
+            more(hi, 0, s)
+            return carry
+
+        lax.fori_loop(P_FIRST, subs, body, 0)
+
+    last = n_h - 1
+    lax.fori_loop(0, last, p_first_step, 0)
+    other_place(0)
+
+    lax.fori_loop(items - group, items, own_step, 0)
+    p_first_step(last, 0)
 
     own0 = at(n_h - 1, 1, 0)
     lanes = down.astype(f32).T.astype(bf16)
@@ -206,57 +255,20 @@
     for d in range(1, n_dp):
         pair_copy(core, lax.rem(core + d, n_dp)).start()
 
-    def add_first(hi, pi, s):
-        item = at(hi, pi, s)
-        first_copy(item).wait_recv()
-        return acc[item] + recv1[item].astype(f32)
-
-    def pass_second(hi, s):
-        send2[hi * subs + s] = add_first(hi, 0, s).astype(bf16)
-        second_copy(hi, s).start()
-
-    def add_second(hi, s, value):
-        second_copy(hi, s).wait_recv()
-        return value + recv2[hi * subs + s].astype(f32)
-
-    def pass_third(hi, s, value):
-        send3[hi * subs + s] = value.astype(bf16)
-        third_copy(hi, s).start()
-
-    def more(hi, pi, s):
-        nxt = at(hi, pi, s) + AHEAD * subs
-
-        @pl.when(nxt < items)
-        def _():
-            first_copy(nxt).start()
-
-    def p_first_step(hi, carry):
-        for s in range(P_FIRST):
-            pass_second(hi, s)
-            acc[at(hi, 1, s)] = add_first(hi, 1, s)
-        return carry
-
-    lax.fori_loop(0, n_h, p_first_step, 0)
-
     def far_step(hi, carry):
-        def other_place(s, c):
-            pass_second(hi, s)
-            more(hi, 0, s)
-            return c
-
         def own_place(s, c):
             value = add_first(hi, 1, s)
             more(hi, 1, s)
             pass_third(hi, s, add_second(hi, s, value))
             return c
 
-        lax.fori_loop(P_FIRST, subs, other_place, 0)
         lax.fori_loop(P_FIRST, subs, own_place, 0)
         for s in range(P_FIRST):
             pass_third(hi, s, add_second(hi, s, acc[at(hi, 1, s)]))
-        return carry
-
-    lax.fori_loop(0, n_h - 1, far_step, 0)
+        other_place(hi + 1)
+        return carry
+
+    lax.fori_loop(0, last, far_step, 0)
 
     for d in range(1, n_dp):
         other = lax.rem(core + d, n_dp)
@@ -267,14 +279,6 @@
     scale = 1.0 / (n_dp * PACK_RECORDS)
     ga_ref[...] = both[:rank] * scale
     gb_ref[...] = both[rank:] * scale
-
-    last = n_h - 1
-
-    def last_other(s, carry):
-        pass_second(last, s)
-        return carry
-
-    lax.fori_loop(P_FIRST, subs, last_other, 0)
 
     for s in range(subs):
         value = acc[own0 + s] if s < P_FIRST else add_first(last, 1, s)

time: 147 us -> 147 us (level)
  no operation moved by 1% of the time
where the time goes in v3:
time: 147 us
  Pallas kernels  142 us (97%)
  local copies, waits for them, and re-layouts  3.98 us (3%)
    pallas_call x1, Pallas kernels, local(): pl.pallas_call(functools.partial(kernel, n_tp, n_dp, clip, cw), out_shape...  142 us
    unnamed x7, local copies, waits for them, and re-layouts  3.98 us

profile of v3, /device:TPU:0, one launch (start us, length us, event | category | flops | bytes accessed | tf_op | source)
XLA Modules:
  0.0 146.7 jit_solution(16052251507234173785)
XLA Ops:
  0.6 142.0 %shard_map.85 = (bf16[512,1536]{1,0:T(8,128)(2,1)}, f32[16,1536]{1,0:T(8,128)}, f32[16,1536]{1,0:T(8,128)}) custom-call(bf16[512,1536]{1,0:T(8,128)(2,1)} %bitcast.5, bf16[512,1536]{1,0:T(8,128)(2,1)} %bitcast.6, s32[1,512]{1,0:T(1,128)} %idx_ref.1, bf16[1536,12288]{1,0:T(8,128)(2,1)} %wq_ref.1, bf16[16,1536]{1,0:T(8,128)(2,1)} %bitcast.7, ...), custom_call_target="tpu_custom_call" | custom-call | flops 19327352832 | bytes 37748736 | tf_op jit(solution)/shard_map/pallas_call | solution.py:331
  142.7 0.0 copy-start.1
  142.7 0.0 copy-start
  142.7 2.7 %copy.12 = bf16[1,512,1536]{2,1,0:T(8,128)(2,1)} copy(bf16[1,512,1536]{2,1,0:T(8,128)(2,1)} %bitcast.4) | data formatting | bytes 3145728
  145.4 0.0 copy-done.1
  145.4 0.6 copy.13
  146.0 0.0 copy-done
  146.0 0.6 copy.14
Async XLA Ops:
  142.7 2.7 %copy-start.1 = (f32[16,1536]{1,0:T(8,128)S(1)}, f32[16,1536]{1,0:T(8,128)}, u32[]{:S(2)}) copy-start(f32[16,1536]{1,0:T(8,128)} %get-tuple-element.13) | copy-start | bytes 294916
  142.7 3.3 %copy-start = (f32[16,1536]{1,0:T(8,128)S(1)}, f32[16,1536]{1,0:T(8,128)}, u32[]{:S(2)}) copy-start(f32[16,1536]{1,0:T(8,128)} %get-tuple-element.14) | copy-start | bytes 294916
